TPU v7x, 512 devices: a whole 4x4x16 slice. The times are simulated.
512 devices in a mesh: gz: 16 (over x, y), ta: 32 (over z, core).
Axes of the slice: x: 4, y: 4, z: 16, core: 2. Of those that a mesh axis runs over, the one named last changes fastest.
Arguments:
- links: float32 [4, 18, 32, 32, 1024], P(None, None, 'gz', 'ta'), may hold values from -1 to 1, as said below
Outputs:
- fixed_links: float32 [4, 18, 32, 32, 1024], P(None, None, 'gz', 'ta')
Inputs may be any that keep to these rules, and one draw needn't show every extreme that they name: `links`: every link is a special unitary 3 by 3 matrix.
All inputs are finite; a program needn't handle non-finite values.
Results may differ from a plain program's by a relative error of at most 0.0001.
Values sent between devices are 32-bit elements; how exact they have to be, the bound alone decides.
A program may use at most 64 MiB of HBM per device.

v0:
```python
import functools
import math

import jax
import jax.numpy as jnp
import numpy as np
from jax import lax
from jax.experimental import pallas as pl
from jax.experimental.pallas import tpu as pltpu
from jax.sharding import PartitionSpec as P

ITERS = 2
STEP_SIZE = 0.08
LINE = 32
GZ = 16
TA = 32
PAIRS = ((0, 1), (0, 2), (1, 2))
LOGICAL = pl.DeviceIdType.LOGICAL
F32 = jnp.float32
BF16 = jnp.bfloat16


def halves(table):
    high = table.astype(jnp.bfloat16)
    return high, (table - high.astype(np.float64)).astype(jnp.bfloat16)


def tables():
    phase = 2.0 * np.pi * (np.outer(np.arange(LINE), np.arange(LINE)) % LINE) / LINE
    plane = np.kron(np.eye(4), (np.cos(phase) + np.sin(phase)) / np.sqrt(LINE))
    sines = 4.0 * np.sin(np.pi * np.arange(LINE) / LINE) ** 2
    row = np.arange(128)
    momenta = sines[row // 8 + 16 * (row % 2)][:, None] + np.tile(sines, 4)[None, :]
    tiles = np.broadcast_to(sines[:, None, None], (LINE, 8, 128))
    return (
        np.concatenate(halves(plane), axis=0),
        momenta.reshape(16, 8, 128).astype(np.float32),
        np.ascontiguousarray(tiles).astype(np.float32),
    )


def times(u, v):
    return (u[0] * v[0] - u[1] * v[1], u[0] * v[1] + u[1] * v[0])


def times_conj(u, v):
    return (u[0] * v[0] + u[1] * v[1], u[1] * v[0] - u[0] * v[1])


def plus(u, v):
    return (u[0] + v[0], u[1] + v[1])


def minus(u, v):
    return (u[0] - v[0], u[1] - v[1])


def conj(u):
    return (u[0], -u[1])


def scaled(u, factor):
    return (u[0] * factor, u[1] * factor)


def total(terms):
    return functools.reduce(plus, terms)


def product(left, right):
    return [[total([times(left[a][j], right[j][b]) for j in range(3)]) for b in range(3)] for a in range(len(left))]


def product_dagger(left, right):
    return [[total([times_conj(left[a][j], right[b][j]) for j in range(3)]) for b in range(3)] for a in range(len(left))]


def cross_conj(u, v):
    row = []
    for c in range(3):
        n, m = (c + 1) % 3, (c + 2) % 3
        row.append(conj(minus(times(u[n], v[m]), times(u[m], v[n]))))
    return row


def each(function, matrix):
    return [[(function(e[0]), function(e[1])) for e in row] for row in matrix]


def lanes(v):
    return lax.broadcasted_iota(jnp.int32, v.shape, v.ndim - 1)


def roll(v, shift, axis):
    return pltpu.roll(v, shift, axis)


def behind_x(v):
    moved = roll(v, 32, v.ndim - 1)
    return jnp.where(lanes(v) < 32, roll(moved, 1, v.ndim - 2), moved)


def ahead_x(v):
    moved = roll(v, 96, v.ndim - 1)
    return jnp.where(lanes(v) >= 96, roll(moved, 7, v.ndim - 2), moved)


def behind_y(v):
    return jnp.where(lanes(v) % 32 == 0, roll(v, 97, v.ndim - 1), roll(v, 1, v.ndim - 1))


def ahead_y(v):
    return jnp.where(lanes(v) % 32 == 31, roll(v, 31, v.ndim - 1), roll(v, 127, v.ndim - 1))


def behind_z(v, edge):
    return jnp.concatenate([edge[None], v[:1]], axis=0)


def ahead_z(v, edge):
    return jnp.concatenate([v[1:], edge[None]], axis=0)


def projected(u):
    third = (u[0][0][1] + u[1][1][1] + u[2][2][1]) * (1.0 / 3.0)
    return (
        [u[a][b][0] - u[b][a][0] for a, b in PAIRS]
        + [u[a][b][1] + u[b][a][1] for a, b in PAIRS]
        + [u[0][0][1] - third, u[1][1][1] - third]
    )


def block_transpose(planes):
    lane = lanes(planes[0])
    axis = planes[0].ndim - 1
    low = lane < 64
    even = (lane // 32) % 2 == 0
    first = [jnp.where(low, planes[p], roll(planes[p + 2], 64, axis)) for p in range(2)]
    second = [jnp.where(low, roll(planes[p], 64, axis), planes[p + 2]) for p in range(2)]
    out = []
    for one, two in (first, second):
        out.append(jnp.where(even, one, roll(two, 32, axis)))
        out.append(jnp.where(even, roll(one, 96, axis), two))
    return out


def rows_of(v):
    return lax.broadcasted_iota(jnp.int32, v.shape, v.ndim - 2)


def bit_exchange(one, two, stride):
    clear = lax.rem(lax.div(rows_of(one), stride), 2) == 0
    return (
        jnp.where(clear, one, roll(two, stride, one.ndim - 2)),
        jnp.where(clear, roll(one, 8 - stride, one.ndim - 2), two),
    )


def middle_exchange(v):
    pair = lax.div(rows_of(v), 2)
    return jnp.where(pair == 1, roll(v, 6, 0), jnp.where(pair == 2, roll(v, 2, 0), v))


def hartley(v):
    size = len(v)
    if size == 1:
        return v
    even, odd = hartley(v[0::2]), hartley(v[1::2])
    half = size // 2
    out = [None] * size
    for k in range(half):
        turned = odd[k]
        if k and 4 * k != size:
            angle = 2.0 * math.pi * k / size
            turned = odd[k] * math.cos(angle) + odd[half - k] * math.sin(angle)
        out[k], out[k + half] = even[k] + turned, even[k] - turned
    return out


def bit_clear(v, stride):
    return lax.rem(lax.div(rows_of(v), stride), 2) == 0


def rotated(v, stride):
    low = bit_clear(v[0], stride)
    out = list(v)
    for k in range(1, 16):
        if k != 8:
            angle = math.pi * k / 16
            out[k] = v[k] * jnp.where(low, 1.0, math.cos(angle)) + v[16 - k] * jnp.where(low, 0.0, math.sin(angle))
    return out


def butterflies(v, stride):
    low = bit_clear(v[0], stride)
    out = []
    for e in v:
        other = roll(e, stride, 0)
        if stride != 4:
            other = jnp.where(low, roll(e, 8 - stride, 0), other)
        out.append(other + jnp.where(low, e, -e))
    return out


def fine_to_coarse(v, stride):
    return butterflies(rotated(hartley(v), stride), stride)


def coarse_to_fine(v, stride):
    return hartley(rotated(butterflies(v, stride), stride))


def tiles_of(matrix):
    return [matrix[8 * i : 8 * i + 8] for i in range(16)]


def plane_forward(fields, table):
    parts = [block_transpose(fields[tl]) for tl in range(2)]
    tiles = [None] * 16
    for b in range(4):
        traded = [bit_exchange(parts[tl][b][0], parts[tl][b][1], 2) for tl in range(2)]
        for bit in range(2):
            tiles[8 * bit + b], tiles[8 * bit + 4 + b] = bit_exchange(traded[0][bit], traded[1][bit], 1)
    tiles = [middle_exchange(v) for v in coarse_to_fine(tiles, 4)]
    return tiles if table is None else right(jnp.concatenate(tiles, axis=0), table)


def plane_inverse(matrix, table):
    tiles = fine_to_coarse([middle_exchange(v) for v in tiles_of(right(matrix, table))], 4)
    blocks = [[None] * 4 for _ in range(2)]
    for b in range(4):
        pairs = [bit_exchange(tiles[8 * bit + b], tiles[8 * bit + 4 + b], 1) for bit in range(2)]
        for tl in range(2):
            blocks[tl][b] = jnp.stack(bit_exchange(pairs[0][tl], pairs[1][tl], 2))
    return [block_transpose(blocks[tl]) for tl in range(2)]


def split(v):
    high = v.astype(BF16)
    return high, (v - high.astype(F32)).astype(BF16)


def right(v, table):
    table_high, table_low = table[pl.ds(0, 128)], table[pl.ds(128, 128)]
    high, low = split(v)
    return jnp.dot(
        jnp.concatenate([high, low, high], axis=1),
        jnp.concatenate([table_high, table_high, table_low], axis=0),
        preferred_element_type=F32,
    )


def store_tiles(ref, tiles):
    for i, tile in enumerate(tiles):
        ref[pl.ds(8 * i, 8)] = tile


def load_tiles(ref):
    return [ref[pl.ds(8 * i, 8)] for i in range(16)]


def inverse_momenta(momenta, tiles):
    row = lax.broadcasted_iota(jnp.int32, (8, 128), 0)
    own = jnp.where(row < 4, tiles[0], tiles[1]) + jnp.where(lax.rem(lax.div(row, 2), 2) == 0, tiles[2], tiles[3])
    squares = momenta + own[None]
    positive = squares > 0.001
    return jnp.where(positive, (16.0 * STEP_SIZE / LINE**3) / jnp.where(positive, squares, 1.0), 0.0).reshape(128, 128)


def normalized(row):
    norm = functools.reduce(jnp.add, [e[0] * e[0] + e[1] * e[1] for e in row])
    scale = lax.rsqrt(norm)
    return [scaled(e, scale) for e in row]


def gauge_rows(fields):
    a, b, c = [(fields[i], fields[3 + i]) for i in range(3)]
    h0, h1 = fields[6], fields[7]
    h2 = -(h0 + h1)
    aa, bb, cc = [e[0] * e[0] + e[1] * e[1] for e in (a, b, c)]
    sixth = 1.0 / 6.0

    def turned(u, h):
        return (-(u[1] * h), u[0] * h)

    s01 = minus(turned(a, -h2), times_conj(b, c))
    s02 = plus(turned(b, -h1), times(a, c))
    s12 = minus(turned(c, -h0), times_conj(b, a))
    d0 = 1.0 - (h0 * h0 + aa + bb) * sixth
    d1 = 1.0 - (h1 * h1 + aa + cc) * sixth
    d2 = 1.0 - (h2 * h2 + bb + cc) * sixth

    def upper(u, s):
        return (0.5 * u[0] + s[0] * sixth, 0.5 * u[1] + s[1] * sixth)

    def lower(u, s):
        return (s[0] * sixth - 0.5 * u[0], 0.5 * u[1] - s[1] * sixth)

    inner = [
        [(d0, 0.5 * h0), upper(a, s01), upper(b, s02)],
        [lower(a, s01), (d1, 0.5 * h1), upper(c, s12)],
        [lower(b, s02), lower(c, s12), (d2, 0.5 * h2)],
    ]
    minus_a = (-a[0], a[1])
    p0 = [total([turned(inner[0][j], h0), times(a, inner[1][j]), times(b, inner[2][j])]) for j in range(3)]
    p1 = [total([times(minus_a, inner[0][j]), turned(inner[1][j], h1), times(c, inner[2][j])]) for j in range(3)]
    p0[0] = (p0[0][0] + 1.0, p0[0][1])
    p1[1] = (p1[1][0] + 1.0, p1[1][1])
    row0 = normalized(p0)
    overlap = total([times_conj(p1[j], row0[j]) for j in range(3)])
    row1 = normalized([minus(p1[j], times(overlap, row0[j])) for j in range(3)])
    return [row0, row1]


def completed(rows):
    return rows + [cross_conj(rows[0], rows[1])]


def load_matrix(ref):
    return [[(ref[2 * (3 * a + b)], ref[2 * (3 * a + b) + 1]) for b in range(3)] for a in range(3)]


def store_matrix(ref, matrix):
    for a, row in enumerate(matrix):
        for b, entry in enumerate(row):
            ref[2 * (3 * a + b)] = entry[0]
            ref[2 * (3 * a + b) + 1] = entry[1]


def load_rows(ref):
    return [[(ref[2 * (3 * a + b)], ref[2 * (3 * a + b) + 1]) for b in range(3)] for a in range(2)]


def kernel(
    links, table_hbm, momenta_hbm, sines_hbm, out,
    u, edge_z, edge_t, sum_send, sums, line_t_send, line_t, line_z_send, line_z, table, momenta, sines, weights,
    plane_send, plane_recv, ring_send, ring_recv, smooth, smooth_za, smooth_zb, smooth_ta, smooth_tb, gauge,
    load_sems, edge_ss, edge_rs, first_ss, first_rs, plane_ss, plane_rs, ring_ss, ring_rs, halo_ss, halo_rs, out_sems,
):
    gz = lax.axis_index("gz")
    ta = lax.axis_index("ta")
    gz_x, gz_y = lax.div(gz, 4), lax.rem(gz, 4)
    chip, core = lax.div(ta, 2), lax.rem(ta, 2)
    other_core = 1 - core

    def device(z, t_chip, which):
        return z * TA + 2 * t_chip + which

    sibling = device(gz, chip, other_core)
    z_next, z_last = lax.rem(gz + 1, GZ), lax.rem(gz + GZ - 1, GZ)
    t_next, t_last = lax.rem(chip + 1, GZ), lax.rem(chip + GZ - 1, GZ)

    def around(place, step, size):
        return lax.rem(place + step, size)

    offsets = [(dx, dy) for dx in range(4) for dy in range(4) if dx or dy]
    offsets.sort(key=lambda o: -(min(o[0], 4 - o[0]) + min(o[1], 4 - o[1])))
    columns = [around(gz_x, dx, 4) for dx in range(4)]
    lines_y = [around(gz_y, dy, 4) for dy in range(4)]
    plane_partners = [(i, device(i, chip, core)) for i in [columns[dx] * 4 + lines_y[dy] for dx, dy in offsets]]
    steps = sorted(range(1, 16), key=lambda d: -min(d, 16 - d))
    ring_partners = [(i, device(gz, i, core)) for i in [around(chip, d, 16) for d in steps]]
    crossed = [
        device(gz, t_last, other_core),
        device(gz, t_next, other_core),
        device(z_last, chip, other_core),
        device(z_next, chip, other_core),
    ]

    barrier = pltpu.get_barrier_semaphore()

    def greet(target):
        pl.semaphore_signal(barrier, inc=1, device_id=target, device_id_type=LOGICAL)

    loads = [pltpu.make_async_copy(links.at[mu], u.at[core, mu], load_sems.at[mu]) for mu in range(4)]
    constants = [
        pltpu.make_async_copy(momenta_hbm, momenta, load_sems.at[4]),
        pltpu.make_async_copy(sines_hbm.at[chip], sines.at[0], load_sems.at[5]),
        pltpu.make_async_copy(sines_hbm.at[chip + 16], sines.at[1], load_sems.at[6]),
        pltpu.make_async_copy(sines_hbm.at[2 * gz], sines.at[2], load_sems.at[7]),
        pltpu.make_async_copy(sines_hbm.at[2 * gz + 1], sines.at[3], load_sems.at[8]),
        pltpu.make_async_copy(table_hbm, table, load_sems.at[9]),
    ]
    for copy in loads[::-1] + constants[-1:]:
        copy.start()
    for _, target in ring_partners + plane_partners:
        greet(target)
    for target in crossed + [sibling]:
        greet(target)
    for copy in constants[:-1]:
        copy.start()

    def transfer(src, dst, send_sem, recv_sem, target):
        return pltpu.make_async_remote_copy(
            src_ref=src, dst_ref=dst, send_sem=send_sem, recv_sem=recv_sem, device_id=target, device_id_type=LOGICAL
        )

    def exchange(sends, recvs, ss, rs, slot, partners, me, neighbour):
        send, recv = sends.at[slot], recvs.at[slot]
        own = pl.ds(pl.multiple_of(me * 8, 8), 8)

        for index, target in partners:
            theirs = pl.ds(pl.multiple_of(index * 8, 8), 8)
            transfer(send.at[theirs], recv.at[own], ss.at[slot], rs.at[slot], target).start()
        recv[own] = send[own]
        part = pl.ds(0, 120)
        return transfer(send.at[part], recv.at[part], ss.at[slot], rs.at[slot], neighbour)

    def plane_exchange(slot):
        neighbour = device(z_next, chip, core)
        return exchange(plane_send, plane_recv, plane_ss, plane_rs, slot, plane_partners, gz, neighbour)

    def ring_exchange(slot):
        neighbour = device(gz, t_next, core)
        return exchange(ring_send, ring_recv, ring_ss, ring_rs, slot, ring_partners, chip, neighbour)

    def halo_transfers(it):
        mine = smooth.at[it, core]
        ss, rs = halo_ss, halo_rs
        to_sibling = transfer(mine, mine, ss.at[it, 0], rs.at[it, 0], sibling)
        groups = []
        for which, (src, dst, z, t_chip) in enumerate(
            (
                (mine.at[0], smooth_ta.at[it, core], gz, t_last),
                (mine.at[:, :, 0], smooth_za.at[it, core], z_last, chip),
                (mine.at[1], smooth_tb.at[it, core], gz, t_next),
                (mine.at[:, :, 1], smooth_zb.at[it, core], z_next, chip),
            )
        ):
            groups.append(
                [
                    transfer(src, dst, ss.at[it, 1 + 2 * which + h], rs.at[it, 1 + which], device(z, t_chip, h))
                    for h in range(2)
                ]
            )
        return to_sibling, groups

    def arrived(it, which, ref):
        transfer(ref.at[it], ref.at[it], halo_ss.at[it, 0], halo_rs.at[it, 1 + which], sibling).wait_recv()

    lane_core = lax.broadcasted_iota(jnp.int32, (8, 128), 0) * 0 + core
    first_half = lane_core == 0

    def own_half(fields):
        return [jnp.where(jnp.broadcast_to(first_half, one.shape), one, two) for one, two in zip(fields[:4], fields[4:])]

    for copy in loads:
        copy.wait()
    lines = [projected(load_matrix(u.at[core, mu])) for mu in range(4)]
    planes = []
    for f in range(8):
        x, y, z, t = [lines[mu][f] for mu in range(4)]
        inner = jnp.concatenate([jnp.zeros((1, 8, 128), F32), z[:1]], axis=0)
        total_here = ((behind_x(x) - x) + (behind_y(y) - y)) + (inner - (z + t))
        planes += [total_here[0], total_here[1], t[0], t[1], z[1]]
    constants[-1].wait()
    planes = right(jnp.concatenate(planes, axis=0), table)
    for f in range(8):
        five = [planes[40 * f + 8 * i : 40 * f + 8 * i + 8] for i in range(5)]
        for z in range(2):
            sum_send[f // 4, f % 4, z] = five[z]
            line_t_send[f // 4, f % 4, z] = five[2 + z]
        line_z_send[f // 4, f % 4] = five[4]
    sums[core] = sum_send[core]

    @pl.when(core == 0)
    def _():
        line_t[1] = line_t_send[0]

    pl.semaphore_wait(barrier, 35)
    sum_out = transfer(sum_send.at[other_core], sums.at[core], first_ss.at[0], first_rs.at[0], sibling)
    sum_in = transfer(sums.at[other_core], sums.at[other_core], first_ss.at[0], first_rs.at[0], sibling)
    t_inner = transfer(line_t_send.at[1], line_t.at[1], first_ss.at[1], first_rs.at[1], sibling)
    t_outer = [
        transfer(line_t_send.at[h], line_t.at[0], first_ss.at[2 + h], first_rs.at[2], device(gz, t_next, h))
        for h in range(2)
    ]
    z_outer = [
        transfer(line_z_send.at[h], line_z.at[core], first_ss.at[4 + h], first_rs.at[3], device(z_next, chip, h))
        for h in range(2)
    ]

    @pl.when(core == 1)
    def _():
        for copy in t_outer:
            copy.start()

    for copy in z_outer:
        copy.start()
    sum_out.start()

    @pl.when(core == 0)
    def _():
        t_inner.start()

    for copy in constants[:-1]:
        copy.wait()
    weights[...] = inverse_momenta(momenta[...], [sines[i] for i in range(4)])
    sum_in.wait_recv()

    @pl.when(core == 1)
    def _():
        t_inner.wait_recv()

    transfer(line_z, line_z, first_ss.at[4], first_rs.at[3], sibling).wait_recv()
    t_outer[0].wait_recv()
    fields = []
    for tl in range(2):
        fields.append([])
        for f in range(4):
            value = sums[tl, f] + line_t[tl, f]
            edge = jnp.stack([line_z[tl, f], jnp.zeros((8, 128), F32)])
            value = value + edge
            factor = 0.5 if f < 2 else jnp.where(jnp.broadcast_to(first_half, value.shape), 0.5, 1.0)
            fields[tl].append(value * factor)
    store_tiles(plane_send.at[0], plane_forward(fields, None))

    to_sibling = [
        transfer(
            links.at[mu, pl.ds(0, 12)], u.at[core, mu, pl.ds(0, 12)], edge_ss.at[5 + mu], edge_rs.at[0], sibling
        )
        for mu in range(4)
    ]
    from_sibling = transfer(
        u.at[other_core, :, pl.ds(0, 12)], u.at[other_core, :, pl.ds(0, 12)], edge_ss.at[0], edge_rs.at[0], sibling
    )
    t_edges = [
        transfer(
            links.at[3, pl.ds(0, 12)], edge_t.at[pl.ds(0, 12)], edge_ss.at[1 + h], edge_rs.at[1], device(gz, t_next, h)
        )
        for h in range(2)
    ]
    z_edges = [
        transfer(
            links.at[2, pl.ds(0, 12), 1], edge_z.at[core, pl.ds(0, 12)], edge_ss.at[3 + h], edge_rs.at[2],
            device(z_next, chip, h),
        )
        for h in range(2)
    ]

    def everything_left():
        sum_out.wait_send()
        for copy in z_outer + z_edges + to_sibling:
            copy.wait_send()

        @pl.when(core == 0)
        def _():
            t_inner.wait_send()

        @pl.when(core == 1)
        def _():
            for copy in t_outer + t_edges:
                copy.wait_send()

        for slot in range(2 * ITERS):
            for send, ss, rs in ((plane_send, plane_ss, plane_rs), (ring_send, ring_ss, ring_rs)):
                part = send.at[slot, pl.ds(0, 120)]
                transfer(part, part, ss.at[slot], rs.at[slot], sibling).wait_send()
        for it in range(ITERS - 1):
            to_other, groups = halo_transfers(it)
            for copy in [to_other] + [copy for group in groups for copy in group]:
                copy.wait_send()

    def beside(it, which):
        if it == 0:
            to_sibling[which].start()
            if which in (1, 2):
                z_edges[which - 1].start()
            else:

                @pl.when(core == 1)
                def _():
                    t_edges[which // 3].start()

    for it in range(ITERS):
        last = it == ITERS - 1
        copy = plane_exchange(2 * it)
        beside(it, 0)
        copy.wait_recv()
        store_tiles(ring_send.at[2 * it], fine_to_coarse(load_tiles(plane_recv.at[2 * it]), 4))
        copy = ring_exchange(2 * it)
        beside(it, 1)
        copy.wait_recv()
        tiles = fine_to_coarse(load_tiles(ring_recv.at[2 * it]), 1)
        tiles = [v * w for v, w in zip(tiles, load_tiles(weights))]
        store_tiles(ring_send.at[2 * it + 1], coarse_to_fine(tiles, 1))
        copy = ring_exchange(2 * it + 1)
        beside(it, 2)
        copy.wait_recv()
        store_tiles(plane_send.at[2 * it + 1], coarse_to_fine(load_tiles(ring_recv.at[2 * it + 1]), 4))
        copy = plane_exchange(2 * it + 1)
        beside(it, 3)
        copy.wait_recv()
        fields = plane_inverse(plane_recv[2 * it + 1], table)
        for tl in range(2):
            for f in range(4):
                smooth[it, core, tl, f] = fields[tl][f]
        to_other, (ahead_t, ahead_z_, after_t, after_z) = halo_transfers(it)
        to_other.start()
        if last:
            ahead_t[1].start()
        else:
            for copy in ahead_t + after_t:
                copy.start()
        for copy in ahead_z_ + ([] if last else after_z):
            copy.start()
        theirs = smooth.at[it, other_core]
        transfer(theirs, theirs, halo_ss.at[it, 0], halo_rs.at[it, 0], sibling).wait_recv()

        def keep(slot, rows):
            for a in range(2):
                for b in range(3):
                    for r in range(2):
                        gauge[slot, 2 * (3 * a + b) + r] = rows[a][b][r]

        for tl in range(2):
            keep(tl, gauge_rows([smooth[it, f // 4, tl, f % 4] for f in range(8)]))

        def turned_inside(where):
            rows = load_rows(gauge.at[where])
            own = completed(rows)
            for mu, shift in ((0, ahead_x), (1, ahead_y)):
                turned = product_dagger(product(rows, load_matrix(u.at[where, mu])), each(shift, own))
                store_matrix(u.at[where, mu], completed(turned))
            for mu in (2, 3):
                store_matrix(u.at[where, mu], product(rows, load_matrix(u.at[where, mu])))

        def turned_z(where, plane, following):
            rows = product_dagger(load_rows(u.at[where, 2, :, plane]), completed(following))
            store_matrix(u.at[where, 2, :, plane], completed(rows))

        def turned_t(where, following):
            rows = product_dagger(load_rows(u.at[where, 3]), completed(load_rows(gauge.at[following])))
            store_matrix(u.at[where, 3], completed(rows))

        def edge_gauges(ref, tl):
            return [[tuple(v[tl] for v in e) for e in row] for row in ref]

        if last:
            outs = [pltpu.make_async_copy(u.at[core, mu], out.at[mu], out_sems.at[mu]) for mu in range(4)]
            turned_inside(core)
            outs[0].start()
            outs[1].start()
            turned_z(core, 0, load_rows(gauge.at[core, :, 1]))
            everything_left()
            arrived(it, 1, smooth_za)
            turned_z(core, 1, gauge_rows([smooth_za[it, f // 4, core, f % 4] for f in range(8)]))
            outs[2].start()

            @pl.when(core == 1)
            def _():
                arrived(it, 0, smooth_ta)
                keep(2, gauge_rows([smooth_ta[it, f // 4, f % 4] for f in range(8)]))

            turned_t(core, core + 1)
            outs[3].start()
        else:
            from_sibling.wait_recv()
            transfer(
                edge_z.at[:, pl.ds(0, 12)], edge_z.at[:, pl.ds(0, 12)], edge_ss.at[0], edge_rs.at[2], sibling
            ).wait_recv()
            t_edges[0].wait_recv()
            missing = [completed(load_rows(u.at[other_core, mu])) for mu in range(4)]
            for mu in range(4):
                store_matrix(u.at[other_core, mu], missing[mu])
            for tl in range(2):
                turned_inside(tl)
            here = [completed(load_rows(gauge.at[tl])) for tl in range(2)]
            store_matrix(edge_t, product_dagger(completed(load_rows(edge_t)), here[0]))
            for tl in range(2):
                edge = product_dagger(completed(load_rows(edge_z.at[tl])), each(lambda v: v[0], here[tl]))
                store_matrix(edge_z.at[tl], edge)
            turned_t(0, 1)
            for tl in range(2):
                turned_z(tl, 0, load_rows(gauge.at[tl, :, 1]))
            even_t = own_half(projected(load_matrix(u.at[0, 3])))
            for tl in range(2):
                x, y = [own_half(projected(load_matrix(u.at[tl, mu]))) for mu in range(2)]
                z = own_half(projected(load_matrix(u.at[tl, 2, :, 0])))
                for f in range(4):
                    value = ((behind_x(x[f]) - x[f]) + (behind_y(y[f]) - y[f])) + jnp.stack([-z[f], z[f]])
                    sums[tl, f] = value + even_t[f] if tl else value - even_t[f]
            arrived(it, 1, smooth_za)
            edges = gauge_rows([smooth_za[it, f // 4, :, f % 4] for f in range(8)])
            for tl in range(2):
                turned_z(tl, 1, edge_gauges(edges, tl))
            arrived(it, 3, smooth_zb)
            edges = gauge_rows([smooth_zb[it, f // 4, :, f % 4] for f in range(8)])
            z_edge = [
                own_half(projected(completed(product(edge_gauges(edges, tl), load_matrix(edge_z.at[tl])))))
                for tl in range(2)
            ]
            z_last_plane = [own_half(projected(load_matrix(u.at[tl, 2, :, 1]))) for tl in range(2)]
            arrived(it, 0, smooth_ta)
            keep(2, gauge_rows([smooth_ta[it, f // 4, f % 4] for f in range(8)]))
            turned_t(1, 2)
            odd_t = own_half(projected(load_matrix(u.at[1, 3])))
            arrived(it, 2, smooth_tb)
            edges = gauge_rows([smooth_tb[it, f // 4, f % 4] for f in range(8)])
            t_edge = own_half(projected(completed(product(edges, load_matrix(edge_t)))))
            fields = []
            for tl in range(2):
                fields.append([])
                for f in range(4):
                    value = sums[tl, f] + jnp.stack([z_edge[tl][f], -z_last_plane[tl][f]])
                    value = value - odd_t[f] if tl else value + t_edge[f]
                    factor = 0.5 if f < 2 else jnp.where(jnp.broadcast_to(first_half, value.shape), 0.5, 1.0)
                    fields[tl].append(value * factor)
            plane_send[2 * it + 2] = plane_forward(fields, table)

    to_other, (ahead_t, ahead_z_, after_t, after_z) = halo_transfers(ITERS - 1)
    for copy in [to_other] + ahead_z_ + ahead_t[1:]:
        copy.wait_send()
    for copy in outs:
        copy.wait()


def shards(links):
    constants = [jnp.asarray(t) for t in tables()]
    anywhere = pl.BlockSpec(memory_space=pl.ANY)
    vmem = pltpu.VMEM
    dma = pltpu.SemaphoreType.DMA
    slots = 2 * ITERS
    result = pl.pallas_call(
        kernel,
        out_shape=pltpu.VMEM((4, 18, 2, 8, 128), F32),
        in_specs=[anywhere] * 4,
        out_specs=anywhere,
        scratch_shapes=[
            vmem((2, 4, 18, 2, 8, 128), F32),
            vmem((2, 18, 8, 128), F32),
            vmem((18, 2, 8, 128), F32),
            vmem((2, 4, 2, 8, 128), F32),
            vmem((2, 4, 2, 8, 128), F32),
            vmem((2, 4, 2, 8, 128), F32),
            vmem((2, 4, 2, 8, 128), F32),
            vmem((2, 4, 8, 128), F32),
            vmem((2, 4, 8, 128), F32),
            vmem((256, 128), BF16),
            vmem((16, 8, 128), F32),
            vmem((4, 8, 128), F32),
            vmem((128, 128), F32),
            vmem((slots, 128, 128), F32),
            vmem((slots, 128, 128), F32),
            vmem((slots, 128, 128), F32),
            vmem((slots, 128, 128), F32),
            vmem((ITERS, 2, 2, 4, 2, 8, 128), F32),
            vmem((ITERS, 2, 2, 4, 8, 128), F32),
            vmem((ITERS, 2, 2, 4, 8, 128), F32),
            vmem((ITERS, 2, 4, 2, 8, 128), F32),
            vmem((ITERS, 2, 4, 2, 8, 128), F32),
            vmem((3, 12, 2, 8, 128), F32),
            dma((10,)),
            dma((9,)),
            dma((3,)),
            dma((6,)),
            dma((4,)),
            dma((slots,)),
            dma((slots,)),
            dma((slots,)),
            dma((slots,)),
            dma((ITERS, 9)),
            dma((ITERS, 5)),
            dma((4,)),
        ],
        compiler_params=pltpu.CompilerParams(
            collective_id=0, has_side_effects=True, vmem_limit_bytes=40 * 1024 * 1024
        ),
    )(*[pltpu.with_memory_space_constraint(a, pltpu.HBM) for a in [links.reshape(4, 18, 2, 8, 128)] + constants])
    return result.reshape(links.shape)


def solution(mesh):
    return jax.shard_map(
        shards,
        mesh=mesh,
        in_specs=(P(None, None, "gz", "ta", None),),
        out_specs=P(None, None, "gz", "ta", None),
        check_vma=False,
    )
```

profile of v0, /device:TPU:1, one launch (start us, length us, event | category | flops | bytes accessed | tf_op | source)
XLA Modules:
  0.0 79.8 jit_solution(8105629532806321156)
XLA Ops:
  0.0 79.0 %shard_map.46 = f32[4,18,2,8,128]{4,3,2,1,0:T(8,128)S(1)} custom-call(f32[4,18,2,8,128]{4,3,2,1,0:T(8,128)} %bitcast.3, bf16[256,128]{1,0:T(8,128)(2,1)} %constant.6.clone.table_hbm, f32[16,8,128]{2,1,0:T(8,128)} %constant.7.clone.momenta_hbm, f32[32,8,128]{2,1,0:T(8,128)} %constant.8.clone.sines_hbm), custom_call_target="tpu_custom_call" | custom-call | tf_op jit(solution)/shard_map/pallas_call | solution.py:724
  79.0 0.8 %copy.7 = f32[4,18,2,1,1024]{4,3,2,1,0:T(1,128)} copy(f32[4,18,2,1,1024]{4,3,2,1,0:T(1,128)S(1)} %bitcast.2) | data formatting | bytes 1179648
where the time goes:
time: 80 us; the launch traced here: 79.8 us
  Pallas kernels  79 us (99%)
  local copies, waits for them, and re-layouts  0.82 us (1%)
    pallas_call x1, Pallas kernels, shards(): pl.pallas_call(kernel, out_shape=pltpu.VMEM((4, 18, 2, 8, 128), F32), in_...  79 us

commit v1 on v0

--- a/solution.py
+++ b/solution.py
@@ -433,6 +433,14 @@
                     for h in range(2)
                 ]
             )
+        if it == ITERS - 1:
+            groups[1] = [
+                transfer(
+                    mine.at[h, :, 0], smooth_za.at[it, core, h], ss.at[it, 3 + h], rs.at[it, 2],
+                    device(z_last, chip, h),
+                )
+                for h in range(2)
+            ]
         return to_sibling, groups
 
     def arrived(it, which, ref):
@@ -596,7 +604,6 @@
             for f in range(4):
                 smooth[it, core, tl, f] = fields[tl][f]
         to_other, (ahead_t, ahead_z_, after_t, after_z) = halo_transfers(it)
-        to_other.start()
         if last:
             ahead_t[1].start()
         else:
@@ -604,6 +611,7 @@
                 copy.start()
         for copy in ahead_z_ + ([] if last else after_z):
             copy.start()
+        to_other.start()
         theirs = smooth.at[it, other_core]
         transfer(theirs, theirs, halo_ss.at[it, 0], halo_rs.at[it, 0], sibling).wait_recv()
 
@@ -643,7 +651,8 @@
             outs[1].start()
             turned_z(core, 0, load_rows(gauge.at[core, :, 1]))
             everything_left()
-            arrived(it, 1, smooth_za)
+            part = smooth_za.at[it, :, core]
+            transfer(part, part, halo_ss.at[it, 0], halo_rs.at[it, 2], sibling).wait_recv()
             turned_z(core, 1, gauge_rows([smooth_za[it, f // 4, core, f % 4] for f in range(8)]))
             outs[2].start()
 

time: 80 us -> 79.7 us (level)
  no operation moved by 1% of the time
where the time goes in v1:
time: 79.7 us; the launch traced here: 79.5 us
  Pallas kernels  78.7 us (99%)
  local copies, waits for them, and re-layouts  0.82 us (1%)
    pallas_call x1, Pallas kernels, shards(): pl.pallas_call(kernel, out_shape=pltpu.VMEM((4, 18, 2, 8, 128), F32), in_...  78.7 us

profile of v1, /device:TPU:1, one launch (start us, length us, event | category | flops | bytes accessed | tf_op | source)
XLA Modules:
  0.0 79.5 jit_solution(10929370263266461991)
XLA Ops:
  0.0 78.7 %shard_map.46 = f32[4,18,2,8,128]{4,3,2,1,0:T(8,128)S(1)} custom-call(f32[4,18,2,8,128]{4,3,2,1,0:T(8,128)} %bitcast.3, bf16[256,128]{1,0:T(8,128)(2,1)} %constant.6.clone.table_hbm, f32[16,8,128]{2,1,0:T(8,128)} %constant.7.clone.momenta_hbm, f32[32,8,128]{2,1,0:T(8,128)} %constant.8.clone.sines_hbm), custom_call_target="tpu_custom_call" | custom-call | tf_op jit(solution)/shard_map/pallas_call | solution.py:733
  78.7 0.8 %copy.7 = f32[4,18,2,1,1024]{4,3,2,1,0:T(1,128)} copy(f32[4,18,2,1,1024]{4,3,2,1,0:T(1,128)S(1)} %bitcast.2) | data formatting | bytes 1179648

commit v2 on v1

--- a/solution.py
+++ b/solution.py
@@ -335,7 +335,7 @@
     links, table_hbm, momenta_hbm, sines_hbm, out,
     u, edge_z, edge_t, sum_send, sums, line_t_send, line_t, line_z_send, line_z, table, momenta, sines, weights,
     plane_send, plane_recv, ring_send, ring_recv, smooth, smooth_za, smooth_zb, smooth_ta, smooth_tb, gauge,
-    load_sems, edge_ss, edge_rs, first_ss, first_rs, plane_ss, plane_rs, ring_ss, ring_rs, halo_ss, halo_rs, out_sems,
+    load_sems, edge_ss, edge_rs, first_ss, first_rs, plane_ss, plane_rs, ring_ss, ring_rs, halo_ss, halo_rs,
 ):
     gz = lax.axis_index("gz")
     ta = lax.axis_index("ta")
@@ -624,45 +624,40 @@
         for tl in range(2):
             keep(tl, gauge_rows([smooth[it, f // 4, tl, f % 4] for f in range(8)]))
 
-        def turned_inside(where):
+        def turned_inside(where, target):
             rows = load_rows(gauge.at[where])
             own = completed(rows)
             for mu, shift in ((0, ahead_x), (1, ahead_y)):
                 turned = product_dagger(product(rows, load_matrix(u.at[where, mu])), each(shift, own))
-                store_matrix(u.at[where, mu], completed(turned))
+                store_matrix(target.at[mu], completed(turned))
             for mu in (2, 3):
                 store_matrix(u.at[where, mu], product(rows, load_matrix(u.at[where, mu])))
 
-        def turned_z(where, plane, following):
+        def turned_z(where, target, plane, following):
             rows = product_dagger(load_rows(u.at[where, 2, :, plane]), completed(following))
-            store_matrix(u.at[where, 2, :, plane], completed(rows))
-
-        def turned_t(where, following):
+            store_matrix(target.at[2, :, plane], completed(rows))
+
+        def turned_t(where, target, following):
             rows = product_dagger(load_rows(u.at[where, 3]), completed(load_rows(gauge.at[following])))
-            store_matrix(u.at[where, 3], completed(rows))
+            store_matrix(target.at[3], completed(rows))
 
         def edge_gauges(ref, tl):
             return [[tuple(v[tl] for v in e) for e in row] for row in ref]
 
         if last:
-            outs = [pltpu.make_async_copy(u.at[core, mu], out.at[mu], out_sems.at[mu]) for mu in range(4)]
-            turned_inside(core)
-            outs[0].start()
-            outs[1].start()
-            turned_z(core, 0, load_rows(gauge.at[core, :, 1]))
+            turned_inside(core, out)
+            turned_z(core, out, 0, load_rows(gauge.at[core, :, 1]))
             everything_left()
             part = smooth_za.at[it, :, core]
             transfer(part, part, halo_ss.at[it, 0], halo_rs.at[it, 2], sibling).wait_recv()
-            turned_z(core, 1, gauge_rows([smooth_za[it, f // 4, core, f % 4] for f in range(8)]))
-            outs[2].start()
+            turned_z(core, out, 1, gauge_rows([smooth_za[it, f // 4, core, f % 4] for f in range(8)]))
 
             @pl.when(core == 1)
             def _():
                 arrived(it, 0, smooth_ta)
                 keep(2, gauge_rows([smooth_ta[it, f // 4, f % 4] for f in range(8)]))
 
-            turned_t(core, core + 1)
-            outs[3].start()
+            turned_t(core, out, core + 1)
         else:
             from_sibling.wait_recv()
             transfer(
@@ -673,15 +668,15 @@
             for mu in range(4):
                 store_matrix(u.at[other_core, mu], missing[mu])
             for tl in range(2):
-                turned_inside(tl)
+                turned_inside(tl, u.at[tl])
             here = [completed(load_rows(gauge.at[tl])) for tl in range(2)]
             store_matrix(edge_t, product_dagger(completed(load_rows(edge_t)), here[0]))
             for tl in range(2):
                 edge = product_dagger(completed(load_rows(edge_z.at[tl])), each(lambda v: v[0], here[tl]))
                 store_matrix(edge_z.at[tl], edge)
-            turned_t(0, 1)
+            turned_t(0, u.at[0], 1)
             for tl in range(2):
-                turned_z(tl, 0, load_rows(gauge.at[tl, :, 1]))
+                turned_z(tl, u.at[tl], 0, load_rows(gauge.at[tl, :, 1]))
             even_t = own_half(projected(load_matrix(u.at[0, 3])))
             for tl in range(2):
                 x, y = [own_half(projected(load_matrix(u.at[tl, mu]))) for mu in range(2)]
@@ -692,7 +687,7 @@
             arrived(it, 1, smooth_za)
             edges = gauge_rows([smooth_za[it, f // 4, :, f % 4] for f in range(8)])
             for tl in range(2):
-                turned_z(tl, 1, edge_gauges(edges, tl))
+                turned_z(tl, u.at[tl], 1, edge_gauges(edges, tl))
             arrived(it, 3, smooth_zb)
             edges = gauge_rows([smooth_zb[it, f // 4, :, f % 4] for f in range(8)])
             z_edge = [
@@ -702,7 +697,7 @@
             z_last_plane = [own_half(projected(load_matrix(u.at[tl, 2, :, 1]))) for tl in range(2)]
             arrived(it, 0, smooth_ta)
             keep(2, gauge_rows([smooth_ta[it, f // 4, f % 4] for f in range(8)]))
-            turned_t(1, 2)
+            turned_t(1, u.at[1], 2)
             odd_t = own_half(projected(load_matrix(u.at[1, 3])))
             arrived(it, 2, smooth_tb)
             edges = gauge_rows([smooth_tb[it, f // 4, f % 4] for f in range(8)])
@@ -720,8 +715,6 @@
     to_other, (ahead_t, ahead_z_, after_t, after_z) = halo_transfers(ITERS - 1)
     for copy in [to_other] + ahead_z_ + ahead_t[1:]:
         copy.wait_send()
-    for copy in outs:
-        copy.wait()
 
 
 def shards(links):
@@ -734,7 +727,7 @@
         kernel,
         out_shape=pltpu.VMEM((4, 18, 2, 8, 128), F32),
         in_specs=[anywhere] * 4,
-        out_specs=anywhere,
+        out_specs=pl.BlockSpec(memory_space=vmem),
         scratch_shapes=[
             vmem((2, 4, 18, 2, 8, 128), F32),
             vmem((2, 18, 8, 128), F32),
@@ -770,7 +763,6 @@
             dma((slots,)),
             dma((ITERS, 9)),
             dma((ITERS, 5)),
-            dma((4,)),
         ],
         compiler_params=pltpu.CompilerParams(
             collective_id=0, has_side_effects=True, vmem_limit_bytes=40 * 1024 * 1024

time: 79.7 us -> 79.4 us (level)
  no operation moved by 1% of the time
where the time goes in v2:
time: 79.4 us; the launch traced here: 79.3 us
  Pallas kernels  78.4 us (99%)
  local copies, waits for them, and re-layouts  0.82 us (1%)
    pallas_call x1, Pallas kernels, shards(): pl.pallas_call(kernel, out_shape=pltpu.VMEM((4, 18, 2, 8, 128), F32), in_...  78.4 us

profile of v2, /device:TPU:1, one launch (start us, length us, event | category | flops | bytes accessed | tf_op | source)
XLA Modules:
  0.0 79.3 jit_solution(10414878742362873349)
XLA Ops:
  0.0 78.4 %shard_map.46 = f32[4,18,2,8,128]{4,3,2,1,0:T(8,128)S(1)} custom-call(f32[4,18,2,8,128]{4,3,2,1,0:T(8,128)} %bitcast.3, bf16[256,128]{1,0:T(8,128)(2,1)} %constant.6.clone.table_hbm, f32[16,8,128]{2,1,0:T(8,128)} %constant.7.clone.momenta_hbm, f32[32,8,128]{2,1,0:T(8,128)} %constant.8.clone.sines_hbm), custom_call_target="tpu_custom_call" | custom-call | tf_op jit(solution)/shard_map/pallas_call | solution.py:726
  78.5 0.8 %copy.7 = f32[4,18,2,1,1024]{4,3,2,1,0:T(1,128)} copy(f32[4,18,2,1,1024]{4,3,2,1,0:T(1,128)S(1)} %bitcast.2) | data formatting | bytes 1179648

commit v3 on v2

--- a/solution.py
+++ b/solution.py
@@ -332,7 +332,7 @@
 
 
 def kernel(
-    links, table_hbm, momenta_hbm, sines_hbm, out,
+    links, table_hbm, momenta_hbm, sines_hbm, out, factor_t, follow_t,
     u, edge_z, edge_t, sum_send, sums, line_t_send, line_t, line_z_send, line_z, table, momenta, sines, weights,
     plane_send, plane_recv, ring_send, ring_recv, smooth, smooth_za, smooth_zb, smooth_ta, smooth_tb, gauge,
     load_sems, edge_ss, edge_rs, first_ss, first_rs, plane_ss, plane_rs, ring_ss, ring_rs, halo_ss, halo_rs,
@@ -616,10 +616,7 @@
         transfer(theirs, theirs, halo_ss.at[it, 0], halo_rs.at[it, 0], sibling).wait_recv()
 
         def keep(slot, rows):
-            for a in range(2):
-                for b in range(3):
-                    for r in range(2):
-                        gauge[slot, 2 * (3 * a + b) + r] = rows[a][b][r]
+            store_matrix(gauge.at[slot], rows)
 
         for tl in range(2):
             keep(tl, gauge_rows([smooth[it, f // 4, tl, f % 4] for f in range(8)]))
@@ -631,7 +628,8 @@
                 turned = product_dagger(product(rows, load_matrix(u.at[where, mu])), each(shift, own))
                 store_matrix(target.at[mu], completed(turned))
             for mu in (2, 3):
-                store_matrix(u.at[where, mu], product(rows, load_matrix(u.at[where, mu])))
+                left = factor_t if last and mu == 3 else u.at[where, mu]
+                store_matrix(left, product(rows, load_matrix(u.at[where, mu])))
 
         def turned_z(where, target, plane, following):
             rows = product_dagger(load_rows(u.at[where, 2, :, plane]), completed(following))
@@ -652,12 +650,14 @@
             transfer(part, part, halo_ss.at[it, 0], halo_rs.at[it, 2], sibling).wait_recv()
             turned_z(core, out, 1, gauge_rows([smooth_za[it, f // 4, core, f % 4] for f in range(8)]))
 
+            @pl.when(core == 0)
+            def _():
+                follow_t[...] = gauge[1]
+
             @pl.when(core == 1)
             def _():
                 arrived(it, 0, smooth_ta)
-                keep(2, gauge_rows([smooth_ta[it, f // 4, f % 4] for f in range(8)]))
-
-            turned_t(core, out, core + 1)
+                store_matrix(follow_t, gauge_rows([smooth_ta[it, f // 4, f % 4] for f in range(8)]))
         else:
             from_sibling.wait_recv()
             transfer(
@@ -717,17 +717,28 @@
         copy.wait_send()
 
 
+def closing_kernel(done, factor_t, follow_t, out, last_links, sems):
+    copies = [pltpu.make_async_copy(done.at[mu], out.at[mu], sems.at[mu]) for mu in range(3)]
+    copies.append(pltpu.make_async_copy(last_links, out.at[3], sems.at[3]))
+    for copy in copies[:3]:
+        copy.start()
+    store_matrix(last_links, completed(product_dagger(load_rows(factor_t), completed(load_rows(follow_t)))))
+    copies[3].start()
+    for copy in copies:
+        copy.wait()
+
+
 def shards(links):
     constants = [jnp.asarray(t) for t in tables()]
     anywhere = pl.BlockSpec(memory_space=pl.ANY)
     vmem = pltpu.VMEM
     dma = pltpu.SemaphoreType.DMA
     slots = 2 * ITERS
-    result = pl.pallas_call(
+    parts = pl.pallas_call(
         kernel,
-        out_shape=pltpu.VMEM((4, 18, 2, 8, 128), F32),
+        out_shape=[vmem((3, 18, 2, 8, 128), F32), vmem((12, 2, 8, 128), F32), vmem((12, 2, 8, 128), F32)],
         in_specs=[anywhere] * 4,
-        out_specs=pl.BlockSpec(memory_space=vmem),
+        out_specs=[pl.BlockSpec(memory_space=vmem)] * 3,
         scratch_shapes=[
             vmem((2, 4, 18, 2, 8, 128), F32),
             vmem((2, 18, 8, 128), F32),
@@ -768,6 +779,14 @@
             collective_id=0, has_side_effects=True, vmem_limit_bytes=40 * 1024 * 1024
         ),
     )(*[pltpu.with_memory_space_constraint(a, pltpu.HBM) for a in [links.reshape(4, 18, 2, 8, 128)] + constants])
+    result = pl.pallas_call(
+        closing_kernel,
+        out_shape=jax.ShapeDtypeStruct((4, 18, 2, 8, 128), F32),
+        in_specs=[pl.BlockSpec(memory_space=vmem)] * 3,
+        out_specs=anywhere,
+        scratch_shapes=[vmem((18, 2, 8, 128), F32), dma((4,))],
+        compiler_params=pltpu.CompilerParams(vmem_limit_bytes=40 * 1024 * 1024),
+    )(*parts)
     return result.reshape(links.shape)
 
 

time: 79.4 us -> 79.4 us (level)
  local copies, waits for them, and re-layouts: 0.82 us -> 0 us
  Pallas kernels: 78.4 us -> 79.2 us
    unnamed x1 -> x0, local copies, waits for them, and re-layouts: 0.82 us -> none
    pallas_call x1 -> x2, Pallas kernels: 78.4 us -> 79.2 us  [the longest x1 78.4 us: shards(): pl.pallas_call(kernel, out_shape=[vmem((3, 18, 2, 8, 128), F32), vmem((12...]
where the time goes in v3:
time: 79.4 us; the launch traced here: 79.2 us
  Pallas kernels  79.2 us (100%)
    pallas_call x1, Pallas kernels, shards(): pl.pallas_call(kernel, out_shape=[vmem((3, 18, 2, 8, 128), F32), vmem((12...  78.4 us

profile of v3, /device:TPU:1, one launch (start us, length us, event | category | flops | bytes accessed | tf_op | source)
XLA Modules:
  0.0 79.2 jit_solution(7428528313914333877)
XLA Ops:
  0.0 78.4 %shard_map.46 = (f32[3,18,2,8,128]{4,3,2,1,0:T(8,128)S(1)}, f32[12,2,8,128]{3,2,1,0:T(8,128)S(1)}, f32[12,2,8,128]{3,2,1,0:T(8,128)S(1)}) custom-call(f32[4,18,2,8,128]{4,3,2,1,0:T(8,128)} %bitcast.2, bf16[256,128]{1,0:T(8,128)(2,1)} %constant.6.clone.table_hbm, f32[16,8,128]{2,1,0:T(8,128)} %constant.7.clone.momenta_hbm, f32[32,8,128]{2,1,0:T(8,128)} %constant.8.clone.sines_hbm), custom_call_target="tpu_custom_call" | custom-call | tf_op jit(solution)/shard_map/pallas_call | solution.py:737
  78.4 0.8 %shard_map.47 = f32[4,18,2,8,128]{4,3,2,1,0:T(8,128)} custom-call(f32[3,18,2,8,128]{4,3,2,1,0:T(8,128)S(1)} %get-tuple-element.8.done, f32[12,2,8,128]{3,2,1,0:T(8,128)S(1)} %get-tuple-element.9.factor_t, f32[12,2,8,128]{3,2,1,0:T(8,128)S(1)} %get-tuple-element.10.follow_t), custom_call_target="tpu_custom_call" | custom-call | tf_op jit(solution)/shard_map/pallas_call | solution.py:782

commit v4 on v3

--- a/solution.py
+++ b/solution.py
@@ -605,13 +605,11 @@
                 smooth[it, core, tl, f] = fields[tl][f]
         to_other, (ahead_t, ahead_z_, after_t, after_z) = halo_transfers(it)
         if last:
-            ahead_t[1].start()
+            order = ahead_z_ + ahead_t[1:] + [to_other]
         else:
-            for copy in ahead_t + after_t:
-                copy.start()
-        for copy in ahead_z_ + ([] if last else after_z):
+            order = ahead_z_ + after_z + [to_other] + ahead_t + after_t
+        for copy in order:
             copy.start()
-        to_other.start()
         theirs = smooth.at[it, other_core]
         transfer(theirs, theirs, halo_ss.at[it, 0], halo_rs.at[it, 0], sibling).wait_recv()
 
@@ -718,12 +716,16 @@
 
 
 def closing_kernel(done, factor_t, follow_t, out, last_links, sems):
-    copies = [pltpu.make_async_copy(done.at[mu], out.at[mu], sems.at[mu]) for mu in range(3)]
-    copies.append(pltpu.make_async_copy(last_links, out.at[3], sems.at[3]))
-    for copy in copies[:3]:
+    pieces = [(mu, pl.ds(9 * half, 9)) for mu in range(4) for half in range(2)]
+    copies = [
+        pltpu.make_async_copy((last_links if mu == 3 else done.at[mu]).at[part], out.at[mu, part], sems.at[i])
+        for i, (mu, part) in enumerate(pieces)
+    ]
+    for copy in copies[:6]:
         copy.start()
     store_matrix(last_links, completed(product_dagger(load_rows(factor_t), completed(load_rows(follow_t)))))
-    copies[3].start()
+    for copy in copies[6:]:
+        copy.start()
     for copy in copies:
         copy.wait()
 
@@ -784,7 +786,7 @@
         out_shape=jax.ShapeDtypeStruct((4, 18, 2, 8, 128), F32),
         in_specs=[pl.BlockSpec(memory_space=vmem)] * 3,
         out_specs=anywhere,
-        scratch_shapes=[vmem((18, 2, 8, 128), F32), dma((4,))],
+        scratch_shapes=[vmem((18, 2, 8, 128), F32), dma((8,))],
         compiler_params=pltpu.CompilerParams(vmem_limit_bytes=40 * 1024 * 1024),
     )(*parts)
     return result.reshape(links.shape)

time: 79.4 us -> 79.4 us (level)
  no operation moved by 1% of the time
where the time goes in v4:
time: 79.4 us; the launch traced here: 79.2 us
  Pallas kernels  79.2 us (100%)
    pallas_call x1, Pallas kernels, shards(): pl.pallas_call(kernel, out_shape=[vmem((3, 18, 2, 8, 128), F32), vmem((12...  78.4 us

profile of v4, /device:TPU:1, one launch (start us, length us, event | category | flops | bytes accessed | tf_op | source)
XLA Modules:
  0.0 79.2 jit_solution(8892593866796514893)
XLA Ops:
  0.0 78.4 %shard_map.46 = (f32[3,18,2,8,128]{4,3,2,1,0:T(8,128)S(1)}, f32[12,2,8,128]{3,2,1,0:T(8,128)S(1)}, f32[12,2,8,128]{3,2,1,0:T(8,128)S(1)}) custom-call(f32[4,18,2,8,128]{4,3,2,1,0:T(8,128)} %bitcast.2, bf16[256,128]{1,0:T(8,128)(2,1)} %constant.6.clone.table_hbm, f32[16,8,128]{2,1,0:T(8,128)} %constant.7.clone.momenta_hbm, f32[32,8,128]{2,1,0:T(8,128)} %constant.8.clone.sines_hbm), custom_call_target="tpu_custom_call" | custom-call | tf_op jit(solution)/shard_map/pallas_call | solution.py:739
  78.4 0.9 %shard_map.47 = f32[4,18,2,8,128]{4,3,2,1,0:T(8,128)} custom-call(f32[3,18,2,8,128]{4,3,2,1,0:T(8,128)S(1)} %get-tuple-element.8.done, f32[12,2,8,128]{3,2,1,0:T(8,128)S(1)} %get-tuple-element.9.factor_t, f32[12,2,8,128]{3,2,1,0:T(8,128)S(1)} %get-tuple-element.10.follow_t), custom_call_target="tpu_custom_call" | custom-call | tf_op jit(solution)/shard_map/pallas_call | solution.py:784

commit v5 on v4

--- a/solution.py
+++ b/solution.py
@@ -355,11 +355,12 @@
 
     offsets = [(dx, dy) for dx in range(4) for dy in range(4) if dx or dy]
     offsets.sort(key=lambda o: -(min(o[0], 4 - o[0]) + min(o[1], 4 - o[1])))
-    columns = [around(gz_x, dx, 4) for dx in range(4)]
-    lines_y = [around(gz_y, dy, 4) for dy in range(4)]
+    sign = 1 - 2 * core
+    columns = [around(gz_x + 4, dx * sign, 4) for dx in range(4)]
+    lines_y = [around(gz_y + 4, dy * sign, 4) for dy in range(4)]
     plane_partners = [(i, device(i, chip, core)) for i in [columns[dx] * 4 + lines_y[dy] for dx, dy in offsets]]
     steps = sorted(range(1, 16), key=lambda d: -min(d, 16 - d))
-    ring_partners = [(i, device(gz, i, core)) for i in [around(chip, d, 16) for d in steps]]
+    ring_partners = [(i, device(gz, i, core)) for i in [around(chip + 16, d * sign, 16) for d in steps]]
     crossed = [
         device(gz, t_last, other_core),
         device(gz, t_next, other_core),
@@ -488,13 +489,14 @@
         for h in range(2)
     ]
 
+    z_outer[0].start()
+
     @pl.when(core == 1)
     def _():
         for copy in t_outer:
             copy.start()
 
-    for copy in z_outer:
-        copy.start()
+    z_outer[1].start()
     sum_out.start()
 
     @pl.when(core == 0)
@@ -604,12 +606,19 @@
             for f in range(4):
                 smooth[it, core, tl, f] = fields[tl][f]
         to_other, (ahead_t, ahead_z_, after_t, after_z) = halo_transfers(it)
-        if last:
-            order = ahead_z_ + ahead_t[1:] + [to_other]
-        else:
-            order = ahead_z_ + after_z + [to_other] + ahead_t + after_t
-        for copy in order:
-            copy.start()
+        for which in range(2):
+            if last:
+                order = [ahead_z_[which], ahead_t[1], ahead_z_[1 - which], to_other]
+            else:
+                links_round = [ahead_z_, ahead_t, after_z, after_t]
+                links_round = links_round[2 * which :] + links_round[: 2 * which]
+                order = [group[0] for group in links_round] + [to_other] + [group[1] for group in links_round]
+
+            @pl.when(core == which)
+            def _():
+                for copy in order:
+                    copy.start()
+
         theirs = smooth.at[it, other_core]
         transfer(theirs, theirs, halo_ss.at[it, 0], halo_rs.at[it, 0], sibling).wait_recv()
 

time: 79.4 us -> 79.7 us (level)
  no operation moved by 1% of the time
where the time goes in v5:
time: 79.7 us; the launch traced here: 79.6 us
  Pallas kernels  79.6 us (100%)
    pallas_call x1, Pallas kernels, shards(): pl.pallas_call(kernel, out_shape=[vmem((3, 18, 2, 8, 128), F32), vmem((12...  78.7 us

profile of v5, /device:TPU:1, one launch (start us, length us, event | category | flops | bytes accessed | tf_op | source)
XLA Modules:
  0.0 79.6 jit_solution(7714593771213263616)
XLA Ops:
  0.0 78.7 %shard_map.46 = (f32[3,18,2,8,128]{4,3,2,1,0:T(8,128)S(1)}, f32[12,2,8,128]{3,2,1,0:T(8,128)S(1)}, f32[12,2,8,128]{3,2,1,0:T(8,128)S(1)}) custom-call(f32[4,18,2,8,128]{4,3,2,1,0:T(8,128)} %bitcast.2, bf16[256,128]{1,0:T(8,128)(2,1)} %constant.6.clone.table_hbm, f32[16,8,128]{2,1,0:T(8,128)} %constant.7.clone.momenta_hbm, f32[32,8,128]{2,1,0:T(8,128)} %constant.8.clone.sines_hbm), custom_call_target="tpu_custom_call" | custom-call | tf_op jit(solution)/shard_map/pallas_call | solution.py:748
  78.7 0.9 %shard_map.47 = f32[4,18,2,8,128]{4,3,2,1,0:T(8,128)} custom-call(f32[3,18,2,8,128]{4,3,2,1,0:T(8,128)S(1)} %get-tuple-element.8.done, f32[12,2,8,128]{3,2,1,0:T(8,128)S(1)} %get-tuple-element.9.factor_t, f32[12,2,8,128]{3,2,1,0:T(8,128)S(1)} %get-tuple-element.10.follow_t), custom_call_target="tpu_custom_call" | custom-call | tf_op jit(solution)/shard_map/pallas_call | solution.py:793

commit v6 on v4

--- a/solution.py
+++ b/solution.py
@@ -607,9 +607,17 @@
         if last:
             order = ahead_z_ + ahead_t[1:] + [to_other]
         else:
-            order = ahead_z_ + after_z + [to_other] + ahead_t + after_t
+            order = [to_other] + ahead_z_ + after_z + ahead_t + after_t
         for copy in order:
             copy.start()
+        if not last:
+            from_sibling.wait_recv()
+            transfer(
+                edge_z.at[:, pl.ds(0, 12)], edge_z.at[:, pl.ds(0, 12)], edge_ss.at[0], edge_rs.at[2], sibling
+            ).wait_recv()
+            t_edges[0].wait_recv()
+            for ref in [u.at[other_core, mu] for mu in range(4)] + [edge_t, edge_z.at[0], edge_z.at[1]]:
+                store_matrix(ref.at[pl.ds(12, 6)], [cross_conj(*load_rows(ref))])
         theirs = smooth.at[it, other_core]
         transfer(theirs, theirs, halo_ss.at[it, 0], halo_rs.at[it, 0], sibling).wait_recv()
 
@@ -657,20 +665,12 @@
                 arrived(it, 0, smooth_ta)
                 store_matrix(follow_t, gauge_rows([smooth_ta[it, f // 4, f % 4] for f in range(8)]))
         else:
-            from_sibling.wait_recv()
-            transfer(
-                edge_z.at[:, pl.ds(0, 12)], edge_z.at[:, pl.ds(0, 12)], edge_ss.at[0], edge_rs.at[2], sibling
-            ).wait_recv()
-            t_edges[0].wait_recv()
-            missing = [completed(load_rows(u.at[other_core, mu])) for mu in range(4)]
-            for mu in range(4):
-                store_matrix(u.at[other_core, mu], missing[mu])
             for tl in range(2):
                 turned_inside(tl, u.at[tl])
             here = [completed(load_rows(gauge.at[tl])) for tl in range(2)]
-            store_matrix(edge_t, product_dagger(completed(load_rows(edge_t)), here[0]))
+            store_matrix(edge_t, product_dagger(load_matrix(edge_t), here[0]))
             for tl in range(2):
-                edge = product_dagger(completed(load_rows(edge_z.at[tl])), each(lambda v: v[0], here[tl]))
+                edge = product_dagger(load_matrix(edge_z.at[tl]), each(lambda v: v[0], here[tl]))
                 store_matrix(edge_z.at[tl], edge)
             turned_t(0, u.at[0], 1)
             for tl in range(2):

time: 79.4 us -> 79.4 us (level)
  no operation moved by 1% of the time
where the time goes in v6:
time: 79.4 us; the launch traced here: 79.2 us
  Pallas kernels  79.2 us (100%)
    pallas_call x1, Pallas kernels, shards(): pl.pallas_call(kernel, out_shape=[vmem((3, 18, 2, 8, 128), F32), vmem((12...  78.4 us

profile of v6, /device:TPU:1, one launch (start us, length us, event | category | flops | bytes accessed | tf_op | source)
XLA Modules:
  0.0 79.2 jit_solution(1340364537852626309)
XLA Ops:
  0.0 78.4 %shard_map.46 = (f32[3,18,2,8,128]{4,3,2,1,0:T(8,128)S(1)}, f32[12,2,8,128]{3,2,1,0:T(8,128)S(1)}, f32[12,2,8,128]{3,2,1,0:T(8,128)S(1)}) custom-call(f32[4,18,2,8,128]{4,3,2,1,0:T(8,128)} %bitcast.2, bf16[256,128]{1,0:T(8,128)(2,1)} %constant.6.clone.table_hbm, f32[16,8,128]{2,1,0:T(8,128)} %constant.7.clone.momenta_hbm, f32[32,8,128]{2,1,0:T(8,128)} %constant.8.clone.sines_hbm), custom_call_target="tpu_custom_call" | custom-call | tf_op jit(solution)/shard_map/pallas_call | solution.py:739
  78.4 0.9 %shard_map.47 = f32[4,18,2,8,128]{4,3,2,1,0:T(8,128)} custom-call(f32[3,18,2,8,128]{4,3,2,1,0:T(8,128)S(1)} %get-tuple-element.8.done, f32[12,2,8,128]{3,2,1,0:T(8,128)S(1)} %get-tuple-element.9.factor_t, f32[12,2,8,128]{3,2,1,0:T(8,128)S(1)} %get-tuple-element.10.follow_t), custom_call_target="tpu_custom_call" | custom-call | tf_op jit(solution)/shard_map/pallas_call | solution.py:784

commit v7 on v6

--- a/solution.py
+++ b/solution.py
@@ -607,7 +607,7 @@
         if last:
             order = ahead_z_ + ahead_t[1:] + [to_other]
         else:
-            order = [to_other] + ahead_z_ + after_z + ahead_t + after_t
+            order = ahead_z_ + after_z + ahead_t + after_t + [to_other]
         for copy in order:
             copy.start()
         if not last:

time: 79.4 us -> 79.4 us (level)
  no operation moved by 1% of the time
where the time goes in v7:
time: 79.4 us; the launch traced here: 79.2 us
  Pallas kernels  79.2 us (100%)
    pallas_call x1, Pallas kernels, shards(): pl.pallas_call(kernel, out_shape=[vmem((3, 18, 2, 8, 128), F32), vmem((12...  78.4 us

profile of v7, /device:TPU:1, one launch (start us, length us, event | category | flops | bytes accessed | tf_op | source)
XLA Modules:
  0.0 79.2 jit_solution(15718150741531202418)
XLA Ops:
  0.0 78.4 %shard_map.46 = (f32[3,18,2,8,128]{4,3,2,1,0:T(8,128)S(1)}, f32[12,2,8,128]{3,2,1,0:T(8,128)S(1)}, f32[12,2,8,128]{3,2,1,0:T(8,128)S(1)}) custom-call(f32[4,18,2,8,128]{4,3,2,1,0:T(8,128)} %bitcast.2, bf16[256,128]{1,0:T(8,128)(2,1)} %constant.6.clone.table_hbm, f32[16,8,128]{2,1,0:T(8,128)} %constant.7.clone.momenta_hbm, f32[32,8,128]{2,1,0:T(8,128)} %constant.8.clone.sines_hbm), custom_call_target="tpu_custom_call" | custom-call | tf_op jit(solution)/shard_map/pallas_call | solution.py:739
  78.4 0.9 %shard_map.47 = f32[4,18,2,8,128]{4,3,2,1,0:T(8,128)} custom-call(f32[3,18,2,8,128]{4,3,2,1,0:T(8,128)S(1)} %get-tuple-element.8.done, f32[12,2,8,128]{3,2,1,0:T(8,128)S(1)} %get-tuple-element.9.factor_t, f32[12,2,8,128]{3,2,1,0:T(8,128)S(1)} %get-tuple-element.10.follow_t), custom_call_target="tpu_custom_call" | custom-call | tf_op jit(solution)/shard_map/pallas_call | solution.py:784

commit v8 on v4

--- a/solution.py
+++ b/solution.py
@@ -355,11 +355,12 @@
 
     offsets = [(dx, dy) for dx in range(4) for dy in range(4) if dx or dy]
     offsets.sort(key=lambda o: -(min(o[0], 4 - o[0]) + min(o[1], 4 - o[1])))
-    columns = [around(gz_x, dx, 4) for dx in range(4)]
-    lines_y = [around(gz_y, dy, 4) for dy in range(4)]
+    sign = 1 - 2 * core
+    columns = [around(gz_x + 4, dx * sign, 4) for dx in range(4)]
+    lines_y = [around(gz_y + 4, dy * sign, 4) for dy in range(4)]
     plane_partners = [(i, device(i, chip, core)) for i in [columns[dx] * 4 + lines_y[dy] for dx, dy in offsets]]
     steps = sorted(range(1, 16), key=lambda d: -min(d, 16 - d))
-    ring_partners = [(i, device(gz, i, core)) for i in [around(chip, d, 16) for d in steps]]
+    ring_partners = [(i, device(gz, i, core)) for i in [around(chip + 16, d * sign, 16) for d in steps]]
     crossed = [
         device(gz, t_last, other_core),
         device(gz, t_next, other_core),

time: 79.4 us -> 79.7 us (level)
  no operation moved by 1% of the time
where the time goes in v8:
time: 79.7 us; the launch traced here: 79.6 us
  Pallas kernels  79.6 us (100%)
    pallas_call x1, Pallas kernels, shards(): pl.pallas_call(kernel, out_shape=[vmem((3, 18, 2, 8, 128), F32), vmem((12...  78.7 us

profile of v8, /device:TPU:1, one launch (start us, length us, event | category | flops | bytes accessed | tf_op | source)
XLA Modules:
  0.0 79.6 jit_solution(5111304515326324781)
XLA Ops:
  0.0 78.7 %shard_map.46 = (f32[3,18,2,8,128]{4,3,2,1,0:T(8,128)S(1)}, f32[12,2,8,128]{3,2,1,0:T(8,128)S(1)}, f32[12,2,8,128]{3,2,1,0:T(8,128)S(1)}) custom-call(f32[4,18,2,8,128]{4,3,2,1,0:T(8,128)} %bitcast.2, bf16[256,128]{1,0:T(8,128)(2,1)} %constant.6.clone.table_hbm, f32[16,8,128]{2,1,0:T(8,128)} %constant.7.clone.momenta_hbm, f32[32,8,128]{2,1,0:T(8,128)} %constant.8.clone.sines_hbm), custom_call_target="tpu_custom_call" | custom-call | tf_op jit(solution)/shard_map/pallas_call | solution.py:740
  78.7 0.9 %shard_map.47 = f32[4,18,2,8,128]{4,3,2,1,0:T(8,128)} custom-call(f32[3,18,2,8,128]{4,3,2,1,0:T(8,128)S(1)} %get-tuple-element.8.done, f32[12,2,8,128]{3,2,1,0:T(8,128)S(1)} %get-tuple-element.9.factor_t, f32[12,2,8,128]{3,2,1,0:T(8,128)S(1)} %get-tuple-element.10.follow_t), custom_call_target="tpu_custom_call" | custom-call | tf_op jit(solution)/shard_map/pallas_call | solution.py:785
